TPU v7x, 128 devices: a whole 4x4x4 slice. The times are simulated.
128 devices in a mesh: ctx: 32 (over x, z, y_hi), head: 4 (over y_lo, core).
Axes of the slice: x: 4, y: 4 (y_hi: 2, y_lo: 2; y = y_hi * 2 + y_lo), z: 4, core: 2. Of those that a mesh axis runs over, the one named last changes fastest.
Arguments:
- q_win: bfloat16 [8192, 8192], P('ctx', 'head'), may hold values from -64 to 64
- k_win: bfloat16 [8192, 2048], P('ctx', 'head'), may hold values from -6 to 6
- v_win: bfloat16 [8192, 2048], P('ctx', 'head'), may hold values from -5 to 5
- q_lin: bfloat16 [8192, 8192], P('ctx', 'head'), may hold values from -5 to 5
- k_lin: bfloat16 [8192, 2048], P('ctx', 'head'), may hold values from -5 to 5
- v_lin: bfloat16 [8192, 2048], P('ctx', 'head'), may hold values from -5 to 5
- level_table: float32 [64, 64, 6], P(None, 'head'), may hold values from 0.05 to 0.6
- level_index: int32 [8192], P('ctx'), may hold values from 0 to 63
- q_cross: bfloat16 [8192, 8192], P('ctx', 'head'), may hold values from -64 to 64
- k_shared: bfloat16 [8192, 2048], P('ctx', 'head'), may hold values from -6 to 6
- v_shared: bfloat16 [8192, 2048], P('ctx', 'head'), may hold values from -5 to 5
- head_gain: float32 [64], P('head'), may hold values from 0.5 to 13.5
Outputs:
- attended: bfloat16 [8192, 8192], P('ctx', 'head')
All inputs are finite; a program needn't handle non-finite values.
Results may differ from a plain program's by a relative error of at most 0.008.
Values may be sent and summed in bfloat16 or wider, within the bound.
A program may use at most 192 MiB of HBM per device.

v0:
```python
import jax
import jax.numpy as jnp
from jax import lax
from jax.experimental import pallas as pl
from jax.experimental.pallas import tpu as pltpu
from jax.sharding import PartitionSpec as P

bf16 = jnp.bfloat16
f32 = jnp.float32
TOK = 256
D = 128
HEADS = 16
GROUPS = 4
PER = 4
GC = PER * D
LEVELS = 6
W = 512
CTX = 32
NEG = -1e30
EXP2_SCALE = D**-0.5 * 1.4426950408889634


def dot(a, b, ca, cb, precision=None):
    return lax.dot_general(
        a, b, (((ca,), (cb,)), ((), ())), preferred_element_type=f32, precision=precision
    )


def kernel(
    q_win, k_win, v_win, q_lin, k_lin, v_lin, table, index, q_cross, k_sh, v_sh, gain,
    out,
    ql, kl, vl, qw, wk, wv, qb, kb, vb, ob, cr, acc, mx, comb, lw,
    state, fs, fr, hs, hr,
    in_sem, s1s, s1r, ws, wr, qs, qr, fss, frs, zs, zr, bs, br, rs, rr, hss, hrs,
):
    c = lax.axis_index("ctx")
    h = lax.axis_index("head")
    x, z, yh = c // 8, (c // 2) % 4, c % 2
    ylo, core = h // 2, h % 2
    role_head = ylo * 2 + yh
    mixed = core == yh

    def flip(other):
        even = (x + other) % 2 == 0
        return jnp.where(even, z, 3 - z)

    def remote(src, dst, ssem, rsem, cc, hh):
        return pltpu.make_async_remote_copy(
            src_ref=src, dst_ref=dst, send_sem=ssem, recv_sem=rsem,
            device_id=(cc, hh), device_id_type=pl.DeviceIdType.MESH,
        )

    loads = [
        (k_lin, kl), (v_lin, vl), (q_lin, ql), (k_win, wk.at[2]), (v_win, wv.at[2]), (q_win, qw),
    ]
    loads = [pltpu.make_async_copy(s, d, in_sem.at[i]) for i, (s, d) in enumerate(loads)]
    for copy in loads:
        copy.start()

    barrier = pltpu.get_barrier_semaphore()

    def greet(cc, hh):
        pl.semaphore_signal(
            barrier, inc=1, device_id=(cc, hh), device_id_type=pl.DeviceIdType.MESH
        )

    for j in range(4):
        @pl.when(jnp.logical_not(mixed & (x == j)))
        def _():
            greet(j * 8 + z * 2 + core, role_head)
            greet(j * 8 + flip(j) * 2 + core, role_head)
    for dz in range(1, 4):
        greet(x * 8 + (z + dz) % 4 * 2 + yh, h)
        greet(c, (h + dz) % 4)
    for o in (1, 2):
        greet((c + o) % CTX, h)
        greet((c + CTX - o) % CTX, h)
    for level in range(5):
        bit = 2**level
        greet(c + bit - 2 * bit * ((c // bit) % 2), h)
    pl.semaphore_wait(barrier, jnp.where(mixed, 6, 8) + 6 + 4 + 5)

    def s1_copy(j, kv):
        src = (k_sh, v_sh)[kv].at[:, pl.ds(j * D, D)]
        dst = (kb, vb)[kv].at[x, z, pl.ds(yh * TOK, TOK), :]
        return src, dst

    for j in range(4):
        for kv in range(2):
            src, dst = s1_copy(j, kv)
            local = mixed & (x == j)

            @pl.when(local)
            def _():
                pltpu.make_async_copy(src, dst, s1r.at[kv, j]).start()

            @pl.when(jnp.logical_not(local))
            def _():
                remote(
                    src, dst, s1s.at[kv, j], s1r.at[kv, x], j * 8 + z * 2 + core, role_head
                ).start()

    for o in (1, 2):
        for kv in range(2):
            @pl.when(c + o < CTX)
            def _():
                remote(
                    (k_win, v_win)[kv], (wk, wv)[kv].at[2 - o],
                    ws.at[kv, o - 1], wr.at[kv, o - 1], c + o, h,
                ).start()

    for j in range(4):
        src = q_cross.at[:, pl.ds(j * GC, GC)]
        dst = qb.at[x]
        local = mixed & (x == j)

        @pl.when(local)
        def _():
            pltpu.make_async_copy(src, dst, qr.at[j]).start()

        @pl.when(jnp.logical_not(local))
        def _():
            remote(src, dst, qs.at[j], qr.at[x], j * 8 + flip(j) * 2 + core, role_head).start()

    def partner(level):
        bit = 2**level
        return c + bit - 2 * bit * ((c // bit) % 2)

    def f_copy(level):
        return remote(
            fs.at[level], fr.at[level], fss.at[level], frs.at[level], partner(level), h
        )

    def fenwick(level):
        f_copy(level).wait_recv()
        got = fr[level]
        if level < 4:
            total = state[...] + got.astype(f32)
            state[...] = total
            fs[level + 1] = total.astype(bf16)
            f_copy(level + 1).start()

    loads[0].wait()
    loads[1].wait()
    for g in range(GROUPS):
        own = dot(kl[:, g * D : (g + 1) * D], vl[:, g * D : (g + 1) * D], 0, 0)
        state[g] = own
        fs[0, g] = own.astype(bf16)
    f_copy(0).start()

    hot = (lax.broadcasted_iota(jnp.int32, (64, TOK), 0) == index[...]).astype(f32)
    lw[...] = dot(hot, table[...], 0, 0, lax.Precision.HIGHEST)

    loads[2].wait()
    rows = lax.broadcasted_iota(jnp.int32, (TOK, TOK), 0)
    cols = lax.broadcasted_iota(jnp.int32, (TOK, TOK), 1)
    causal = rows >= cols
    for g in range(GROUPS):
        for r in range(PER):
            hd = g * PER + r
            s = dot(ql[:, hd * D : (hd + 1) * D], kl[:, g * D : (g + 1) * D], 1, 1)
            s = jnp.where(causal, s * (D * TOK) ** -0.5, 0.0).astype(bf16)
            comb[:, hd * D : (hd + 1) * D] = lw[:, hd * LEVELS : hd * LEVELS + 1] * dot(
                s, vl[:, g * D : (g + 1) * D], 1, 0
            )

    def z_copy(kv, chunk, dz):
        part = (kb, vb)[kv].at[chunk, z, pl.ds(core * TOK, TOK), :]
        return remote(
            part, part, zs.at[kv, chunk, dz - 1], zr.at[kv, chunk, dz - 1],
            x * 8 + (z + dz) % 4 * 2 + yh, h,
        )

    def z_start(chunk):
        for kv in range(2):
            part = (kb, vb)[kv].at[chunk, z, pl.ds(core * TOK, TOK), :]
            remote(part, part, s1s.at[kv, 0], s1r.at[kv, chunk], c, h).wait_recv()
        for kv in range(2):
            for dz in (1, 3, 2):
                z_copy(kv, chunk, dz).start()

    def b_copy(kv, chunk):
        part = (kb, vb)[kv].at[chunk, :, pl.ds(core * TOK, TOK), :]
        return remote(part, part, bs.at[kv, chunk], br.at[kv, chunk], c, h + 1 - 2 * core)

    def b_start(chunk):
        for kv in range(2):
            for dz in range(1, 4):
                z_copy(kv, chunk, dz).wait_recv()
            b_copy(kv, chunk).start()

    def b_wait(chunk):
        for kv in range(2):
            b_copy(kv, chunk).wait_recv()

    z_start(0)
    fenwick(0)

    for i in (3, 4, 5):
        loads[i].wait()
    for o in (1, 2):
        for kv in range(2):
            ref = (wk, wv)[kv]

            @pl.when(c - o >= 0)
            def _():
                remote(
                    ref.at[2], ref.at[2 - o], ws.at[kv, o - 1], wr.at[kv, o - 1], c, h
                ).wait_recv()

            @pl.when(c - o < 0)
            def _():
                ref[2 - o] = jnp.zeros((TOK, GROUPS * D), bf16)

    far = 3 * TOK
    row = lax.broadcasted_iota(jnp.int32, (TOK, far), 0) + 2 * TOK
    col = lax.broadcasted_iota(jnp.int32, (TOK, far), 1)
    band = (col <= row) & (col > row - W) & (col >= (2 - c) * TOK)
    ones = jnp.ones((far, D), bf16)

    def window_group(g):
        kk = wk[:, :, g * D : (g + 1) * D].reshape(far, D)
        vv = jnp.concatenate([wv[:, :, g * D : (g + 1) * D].reshape(far, D), ones], axis=1)

        def scores(r):
            hd = g * PER + r
            return dot(qw[:, hd * D : (hd + 1) * D], kk, 1, 1)

        nxt = scores(0)
        for r in range(PER):
            s = nxt
            if r + 1 < PER:
                nxt = scores(r + 1)
            hd = g * PER + r
            s = jnp.where(band, s, NEG)
            top = jnp.max(s, axis=1, keepdims=True)
            p = jnp.exp2(s * EXP2_SCALE - top * EXP2_SCALE).astype(bf16)
            o = dot(p, vv, 1, 0)
            comb[:, hd * D : (hd + 1) * D] += o[:, :D] / o[:, D:]

    window_group(0)
    fenwick(1)
    z_start(1)
    window_group(1)
    fenwick(2)
    b_start(0)
    window_group(2)
    fenwick(3)
    z_start(2)
    window_group(3)
    fenwick(4)
    z_start(3)
    b_start(1)

    for level in range(5):
        scale = jnp.where((c // 2**level) % 2 == 1, (D * TOK * 2**level) ** -0.5, 0.0)
        for g in range(GROUPS):
            bucket = fr[level, g]
            for r in range(PER):
                hd = g * PER + r
                term = dot(ql[:, hd * D : (hd + 1) * D], bucket, 1, 0)
                at = hd * LEVELS + level + 1
                comb[:, hd * D : (hd + 1) * D] += (lw[:, at : at + 1] * scale) * term

    acc[...] = jnp.zeros_like(acc)
    mx[...] = jnp.full_like(mx, NEG)
    for j in range(4):
        remote(q_cross.at[:, pl.ds(0, GC)], qb.at[j], qs.at[j], qr.at[j], c, h).wait_recv()

    def attend(blk, kk, vv, mask):
        size = kk.shape[0]
        vv = jnp.concatenate([vv, jnp.ones((size, D), bf16)], axis=1)

        def scores(r):
            return dot(qb[blk, :, r * D : (r + 1) * D], kk, 1, 1)

        nxt = scores(0)
        for r in range(PER):
            s = nxt
            if r + 1 < PER:
                nxt = scores(r + 1)
            if mask is not None:
                s = jnp.where(mask, s, NEG)
            sl = pl.ds(r * TOK, TOK)
            old = mx[blk, sl, :][:, :1]
            new = jnp.maximum(old, jnp.max(s, axis=1, keepdims=True))
            p = jnp.exp2(s * EXP2_SCALE - new * EXP2_SCALE).astype(bf16)
            damp = jnp.exp2((old - new) * EXP2_SCALE)
            acc[blk, sl, :] = acc[blk, sl, :] * damp + dot(p, vv, 1, 0)
            mx[blk, sl, :] = jnp.broadcast_to(new, (TOK, D))

    half = 1024

    def half_kv(ref, chunk, part):
        return ref[chunk, pl.ds(part * 2, 2)].reshape(half, D)

    def r_copy(blk):
        return remote(
            ob.at[blk], cr.at[x], rs.at[blk], rr.at[x],
            blk * 8 + flip(blk) * 2 + core, role_head,
        )

    def chunk_step(chunk, carry):
        b_wait(chunk)

        @pl.when(chunk < 3)
        def _():
            @pl.when(chunk > 0)
            def _():
                b_start(chunk + 1)

        place = flip(chunk) * 2 + core

        def full_half(part, carry2):
            attend(chunk, half_kv(kb, chunk, part), half_kv(vb, chunk, part), None)
            return carry2

        lax.fori_loop(0, place // 4, full_half, 0)
        part = place // 4
        first = (place % 4) * TOK
        row = lax.broadcasted_iota(jnp.int32, (TOK, half), 0) + first
        col = lax.broadcasted_iota(jnp.int32, (TOK, half), 1)
        attend(chunk, half_kv(kb, chunk, part), half_kv(vb, chunk, part), col <= row)
        for r in range(PER):
            sl = pl.ds(r * TOK, TOK)
            ob[chunk, :, r * D : (r + 1) * D] = (
                acc[chunk, sl, :D] / acc[chunk, sl, D:]
            ).astype(bf16)
        local = mixed & (x == chunk)

        @pl.when(local)
        def _():
            pltpu.make_async_copy(ob.at[chunk], cr.at[x], rr.at[x]).start()

        @pl.when(jnp.logical_not(local))
        def _():
            r_copy(chunk).start()

        def full(blk, carry2):
            attend(blk, kb[chunk].reshape(2048, D), vb[chunk].reshape(2048, D), None)
            return carry2

        lax.fori_loop(chunk + 1, 4, full, 0)
        return carry

    lax.fori_loop(0, 4, chunk_step, 0)

    square = jnp.zeros((TOK, D), f32)
    for j in range(4):
        remote(ob.at[j], cr.at[j], rs.at[j], rr.at[j], c, h).wait_recv()
        for r in range(PER):
            hd = j * PER + r
            at = slice(hd * D, (hd + 1) * D)
            v = (comb[:, at] + cr[j, :, r * D : (r + 1) * D].astype(f32)) * gain[hd]
            comb[:, at] = v
            square += v * v
    hs[...] = dot(jnp.ones((8, D), f32), square, 1, 1, lax.Precision.HIGHEST)
    for d in range(1, 4):
        remote(hs, hr.at[d - 1], hss.at[d - 1], hrs.at[d - 1], c, (h + d) % 4).start()
    total = hs[...]
    for d in range(1, 4):
        remote(hs, hr.at[d - 1], hss.at[d - 1], hrs.at[d - 1], c, (h + d) % 4).wait_recv()
        total = total + hr[d - 1]
    norm = lax.rsqrt(total / (4 * HEADS * D) + 1e-6).T[:, :1]
    for hd in range(HEADS):
        at = slice(hd * D, (hd + 1) * D)
        out[:, at] = (comb[:, at] * norm).astype(bf16)

    for j in range(4):
        local = mixed & (x == j)

        @pl.when(jnp.logical_not(local))
        def _():
            for kv in range(2):
                src, dst = s1_copy(j, kv)
                remote(src, dst, s1s.at[kv, j], s1r.at[kv, x], c, h).wait_send()
            remote(
                q_cross.at[:, pl.ds(j * GC, GC)], qb.at[x], qs.at[j], qr.at[x], c, h
            ).wait_send()
            r_copy(j).wait_send()
        for kv in range(2):
            b_copy(kv, j).wait_send()
            for dz in range(1, 4):
                z_copy(kv, j, dz).wait_send()
    for o in (1, 2):
        for kv in range(2):
            @pl.when(c + o < CTX)
            def _():
                remote(
                    (k_win, v_win)[kv], (wk, wv)[kv].at[2 - o],
                    ws.at[kv, o - 1], wr.at[kv, o - 1], c, h,
                ).wait_send()
    for level in range(5):
        f_copy(level).wait_send()
    for d in range(1, 4):
        remote(hs, hr.at[d - 1], hss.at[d - 1], hrs.at[d - 1], c, h).wait_send()


def per_device(
    q_win, k_win, v_win, q_lin, k_lin, v_lin, level_table, level_index, q_cross, k_shared,
    v_shared, head_gain,
):
    dma = pltpu.SemaphoreType.DMA
    whole = pl.BlockSpec(memory_space=pl.ANY)
    vmem = pl.BlockSpec(memory_space=pltpu.VMEM)
    smem = pl.BlockSpec(memory_space=pltpu.SMEM)
    kv = GROUPS * D
    return pl.pallas_call(
        kernel,
        out_shape=jax.ShapeDtypeStruct((TOK, HEADS * D), bf16),
        in_specs=[whole] * 6 + [vmem, vmem] + [whole] * 3 + [smem],
        out_specs=vmem,
        scratch_shapes=[
            pltpu.VMEM((TOK, HEADS * D), bf16),
            pltpu.VMEM((TOK, kv), bf16),
            pltpu.VMEM((TOK, kv), bf16),
            pltpu.VMEM((TOK, HEADS * D), bf16),
            pltpu.VMEM((3, TOK, kv), bf16),
            pltpu.VMEM((3, TOK, kv), bf16),
            pltpu.VMEM((4, TOK, GC), bf16),
            pltpu.VMEM((4, 4, 2 * TOK, D), bf16),
            pltpu.VMEM((4, 4, 2 * TOK, D), bf16),
            pltpu.VMEM((4, TOK, GC), bf16),
            pltpu.VMEM((4, TOK, GC), bf16),
            pltpu.VMEM((4, PER * TOK, 2 * D), f32),
            pltpu.VMEM((4, PER * TOK, D), f32),
            pltpu.VMEM((TOK, HEADS * D), f32),
            pltpu.VMEM((TOK, HEADS * LEVELS), f32),
            pltpu.VMEM((GROUPS, D, D), f32),
            pltpu.VMEM((5, GROUPS, D, D), bf16),
            pltpu.VMEM((5, GROUPS, D, D), bf16),
            pltpu.VMEM((8, TOK), f32),
            pltpu.VMEM((3, 8, TOK), f32),
            dma((6,)),
            dma((2, 4)), dma((2, 4)),
            dma((2, 2)), dma((2, 2)),
            dma((4,)), dma((4,)),
            dma((5,)), dma((5,)),
            dma((2, 4, 3)), dma((2, 4, 3)),
            dma((2, 4)), dma((2, 4)),
            dma((4,)), dma((4,)),
            dma((3,)), dma((3,)),
        ],
        compiler_params=pltpu.CompilerParams(
            collective_id=0, has_side_effects=True, vmem_limit_bytes=56 * 2**20
        ),
        name="hybrid_attention",
    )(
        q_win, k_win, v_win, q_lin, k_lin, v_lin,
        level_table.reshape(level_table.shape[0], -1), level_index.reshape(1, -1),
        q_cross, k_shared, v_shared, head_gain,
    )


def solution(mesh):
    return jax.shard_map(
        per_device,
        mesh=mesh,
        in_specs=(
            P("ctx", "head"),
            P("ctx", "head"),
            P("ctx", "head"),
            P("ctx", "head"),
            P("ctx", "head"),
            P("ctx", "head"),
            P(None, "head", None),
            P("ctx"),
            P("ctx", "head"),
            P("ctx", "head"),
            P("ctx", "head"),
            P("head"),
        ),
        out_specs=P("ctx", "head"),
        check_vma=False,
    )
```

profile of v0, /device:TPU:7, one launch (start us, length us, event | category | flops | bytes accessed | tf_op | source)
XLA Modules:
  0.0 130.2 jit_solution(1040076162091373154)
XLA Ops:
  0.0 0.8 copy.14
  0.8 0.7 copy.15.table
  1.5 126.4 %hybrid_attention.1 = bf16[256,2048]{1,0:T(8,128)(2,1)} custom-call(bf16[256,2048]{1,0:T(8,128)(2,1)} %q_win.1, bf16[256,512]{1,0:T(8,128)(2,1)} %k_win.1, bf16[256,512]{1,0:T(8,128)(2,1)} %v_win.1, bf16[256,2048]{1,0:T(8,128)(2,1)} %q_lin.1, bf16[256,512]{1,0:T(8,128)(2,1)} %k_lin.1, bf16[256,512]{1,0:T(8,128)(2,1)} %v_lin.1, f32[64,96]{1,0:T(8,128)} %copy.15.table, ...), custom_call_target="tpu_custom_call" | custom-call | tf_op jit(solution)/shard_map/hybrid_attention/pallas_call | solution.py:408
  127.9 2.3 %copy.17 = bf16[256,2048]{1,0:T(8,128)(2,1)} copy(bf16[256,2048]{1,0:T(8,128)(2,1)} %hybrid_attention.1) | data formatting | bytes 2097152
  (1 shorter events, 0.0 us)
where the time goes:
time: 131 us; the launch traced here: 130 us
  Pallas kernels  126 us (96%)
  local copies, waits for them, and re-layouts  3.83 us (3%)
    pallas_call x1, Pallas kernels, per_device(): pl.pallas_call(kernel, out_shape=jax.ShapeDtypeStruct((TOK, HEADS * D), b...  126 us
    unnamed x2, local copies, waits for them, and re-layouts  3.12 us

commit v1 on v0

--- a/solution.py
+++ b/solution.py
@@ -40,10 +40,6 @@
     role_head = ylo * 2 + yh
     mixed = core == yh
 
-    def flip(other):
-        even = (x + other) % 2 == 0
-        return jnp.where(even, z, 3 - z)
-
     def remote(src, dst, ssem, rsem, cc, hh):
         return pltpu.make_async_remote_copy(
             src_ref=src, dst_ref=dst, send_sem=ssem, recv_sem=rsem,
@@ -64,81 +60,32 @@
             barrier, inc=1, device_id=(cc, hh), device_id_type=pl.DeviceIdType.MESH
         )
 
+    def partner(level):
+        bit = 2**level
+        return c + bit - 2 * bit * ((c // bit) % 2)
+
     for j in range(4):
         @pl.when(jnp.logical_not(mixed & (x == j)))
         def _():
             greet(j * 8 + z * 2 + core, role_head)
-            greet(j * 8 + flip(j) * 2 + core, role_head)
+
+    @pl.when(jnp.logical_not(mixed))
+    def _():
+        greet(partner(3), h)
+        greet(partner(4), h)
+
     for dz in range(1, 4):
         greet(x * 8 + (z + dz) % 4 * 2 + yh, h)
         greet(c, (h + dz) % 4)
-    for o in (1, 2):
-        greet((c + o) % CTX, h)
-        greet((c + CTX - o) % CTX, h)
-    for level in range(5):
-        bit = 2**level
-        greet(c + bit - 2 * bit * ((c // bit) % 2), h)
-    pl.semaphore_wait(barrier, jnp.where(mixed, 6, 8) + 6 + 4 + 5)
-
-    def s1_copy(j, kv):
-        src = (k_sh, v_sh)[kv].at[:, pl.ds(j * D, D)]
-        dst = (kb, vb)[kv].at[x, z, pl.ds(yh * TOK, TOK), :]
-        return src, dst
-
-    for j in range(4):
-        for kv in range(2):
-            src, dst = s1_copy(j, kv)
-            local = mixed & (x == j)
-
-            @pl.when(local)
-            def _():
-                pltpu.make_async_copy(src, dst, s1r.at[kv, j]).start()
-
-            @pl.when(jnp.logical_not(local))
-            def _():
-                remote(
-                    src, dst, s1s.at[kv, j], s1r.at[kv, x], j * 8 + z * 2 + core, role_head
-                ).start()
-
-    for o in (1, 2):
-        for kv in range(2):
-            @pl.when(c + o < CTX)
-            def _():
-                remote(
-                    (k_win, v_win)[kv], (wk, wv)[kv].at[2 - o],
-                    ws.at[kv, o - 1], wr.at[kv, o - 1], c + o, h,
-                ).start()
-
-    for j in range(4):
-        src = q_cross.at[:, pl.ds(j * GC, GC)]
-        dst = qb.at[x]
-        local = mixed & (x == j)
-
-        @pl.when(local)
-        def _():
-            pltpu.make_async_copy(src, dst, qr.at[j]).start()
-
-        @pl.when(jnp.logical_not(local))
-        def _():
-            remote(src, dst, qs.at[j], qr.at[x], j * 8 + flip(j) * 2 + core, role_head).start()
-
-    def partner(level):
-        bit = 2**level
-        return c + bit - 2 * bit * ((c // bit) % 2)
-
-    def f_copy(level):
-        return remote(
-            fs.at[level], fr.at[level], fss.at[level], frs.at[level], partner(level), h
-        )
-
-    def fenwick(level):
-        f_copy(level).wait_recv()
-        got = fr[level]
-        if level < 4:
-            total = state[...] + got.astype(f32)
-            state[...] = total
-            fs[level + 1] = total.astype(bf16)
-            f_copy(level + 1).start()
+    greet(partner(0), h)
+
+    @pl.when(z == 3)
+    def _():
+        greet((c + 2) % CTX, h)
+
+    @pl.when(z == 0)
+    def _():
+        greet((c + CTX - 2) % CTX, h)
 
     loads[0].wait()
     loads[1].wait()
@@ -146,7 +93,6 @@
         own = dot(kl[:, g * D : (g + 1) * D], vl[:, g * D : (g + 1) * D], 0, 0)
         state[g] = own
         fs[0, g] = own.astype(bf16)
-    f_copy(0).start()
 
     hot = (lax.broadcasted_iota(jnp.int32, (64, TOK), 0) == index[...]).astype(f32)
     lw[...] = dot(hot, table[...], 0, 0, lax.Precision.HIGHEST)
@@ -164,20 +110,80 @@
                 s, vl[:, g * D : (g + 1) * D], 1, 0
             )
 
-    def z_copy(kv, chunk, dz):
-        part = (kb, vb)[kv].at[chunk, z, pl.ds(core * TOK, TOK), :]
+    pl.semaphore_wait(
+        barrier,
+        jnp.where(mixed, 3, 6) + 7 + jnp.where((z == 0) | (z == 3), 1, 0),
+    )
+
+    def s1_copy(j, kv):
+        src = (k_sh, v_sh)[kv].at[:, pl.ds(j * D, D)]
+        dst = (kb, vb)[kv].at[x, z, pl.ds(yh * TOK, TOK), :]
+        return src, dst
+
+    for j in range(4):
+        for kv in range(2):
+            src, dst = s1_copy(j, kv)
+            local = mixed & (x == j)
+
+            @pl.when(local)
+            def _():
+                pltpu.make_async_copy(src, dst, s1r.at[kv, j]).start()
+
+            @pl.when(jnp.logical_not(local))
+            def _():
+                remote(
+                    src, dst, s1s.at[kv, j], s1r.at[kv, x], j * 8 + z * 2 + core, role_head
+                ).start()
+
+    def f_copy(level):
         return remote(
-            part, part, zs.at[kv, chunk, dz - 1], zr.at[kv, chunk, dz - 1],
-            x * 8 + (z + dz) % 4 * 2 + yh, h,
+            fs.at[level], fr.at[level], fss.at[level], frs.at[level], partner(level), h
+        )
+
+    def fenwick(level):
+        f_copy(level).wait_recv()
+        got = fr[level]
+        if level < 4:
+            total = state[...] + got.astype(f32)
+            state[...] = total
+            fs[level + 1] = total.astype(bf16)
+            f_copy(level + 1).start()
+
+    f_copy(0).start()
+
+    for j in range(4):
+        src = q_cross.at[:, pl.ds(j * GC, GC)]
+        dst = qb.at[x]
+        local = mixed & (x == j)
+
+        @pl.when(local)
+        def _():
+            pltpu.make_async_copy(src, dst, qr.at[j]).start()
+
+        @pl.when(jnp.logical_not(local))
+        def _():
+            remote(src, dst, qs.at[j], qr.at[x], j * 8 + z * 2 + core, role_head).start()
+
+    def z_copy(kv, chunk, step):
+        tile = (z + 1) % 4 if step == 2 else z
+        to = (z + 1) % 4 if step == 0 else (z + 3) % 4
+        part = (kb, vb)[kv].at[chunk, tile, pl.ds(core * TOK, TOK), :]
+        return remote(
+            part, part, zs.at[kv, chunk, step], zr.at[kv, chunk, step],
+            x * 8 + to * 2 + yh, h,
         )
 
     def z_start(chunk):
         for kv in range(2):
             part = (kb, vb)[kv].at[chunk, z, pl.ds(core * TOK, TOK), :]
             remote(part, part, s1s.at[kv, 0], s1r.at[kv, chunk], c, h).wait_recv()
-        for kv in range(2):
-            for dz in (1, 3, 2):
-                z_copy(kv, chunk, dz).start()
+            for step in (1, 0):
+                z_copy(kv, chunk, step).start()
+
+    def z_forward(chunk):
+        for kv in range(2):
+            z_copy(kv, chunk, 1).wait_recv()
+            z_copy(kv, chunk, 2).start()
 
     def b_copy(kv, chunk):
         part = (kb, vb)[kv].at[chunk, :, pl.ds(core * TOK, TOK), :]
@@ -185,82 +191,57 @@
 
     def b_start(chunk):
         for kv in range(2):
-            for dz in range(1, 4):
-                z_copy(kv, chunk, dz).wait_recv()
+            for step in (0, 2):
+                z_copy(kv, chunk, step).wait_recv()
             b_copy(kv, chunk).start()
 
     def b_wait(chunk):
         for kv in range(2):
             b_copy(kv, chunk).wait_recv()
 
+    def w_copy(kv):
+        return remote(
+            (k_win, v_win)[kv], (wk, wv)[kv].at[0], ws.at[kv, 0], wr.at[kv, 0], c + 2, h
+        )
+
+    def w_start():
+        for kv in range(2):
+            @pl.when(c + 2 < CTX)
+            def _():
+                w_copy(kv).start()
+
+    def y_copy(kv, slot):
+        ref = (wk, wv)[kv]
+        return remote(ref.at[slot], ref.at[1], ws.at[kv, 1], wr.at[kv, 1], partner(0), h)
+
+    def w_arrive():
+        for kv in range(2):
+            ref = (wk, wv)[kv]
+
+            @pl.when(c >= 2)
+            def _():
+                w_copy(kv).wait_recv()
+
+            @pl.when(c < 2)
+            def _():
+                ref[0] = jnp.zeros((TOK, GROUPS * D), bf16)
+
+            @pl.when(yh == 1)
+            def _():
+                y_copy(kv, 0).start()
+
     z_start(0)
-    fenwick(0)
-
     for i in (3, 4, 5):
         loads[i].wait()
-    for o in (1, 2):
-        for kv in range(2):
-            ref = (wk, wv)[kv]
-
-            @pl.when(c - o >= 0)
-            def _():
-                remote(
-                    ref.at[2], ref.at[2 - o], ws.at[kv, o - 1], wr.at[kv, o - 1], c, h
-                ).wait_recv()
-
-            @pl.when(c - o < 0)
-            def _():
-                ref[2 - o] = jnp.zeros((TOK, GROUPS * D), bf16)
-
-    far = 3 * TOK
-    row = lax.broadcasted_iota(jnp.int32, (TOK, far), 0) + 2 * TOK
-    col = lax.broadcasted_iota(jnp.int32, (TOK, far), 1)
-    band = (col <= row) & (col > row - W) & (col >= (2 - c) * TOK)
-    ones = jnp.ones((far, D), bf16)
-
-    def window_group(g):
-        kk = wk[:, :, g * D : (g + 1) * D].reshape(far, D)
-        vv = jnp.concatenate([wv[:, :, g * D : (g + 1) * D].reshape(far, D), ones], axis=1)
-
-        def scores(r):
-            hd = g * PER + r
-            return dot(qw[:, hd * D : (hd + 1) * D], kk, 1, 1)
-
-        nxt = scores(0)
-        for r in range(PER):
-            s = nxt
-            if r + 1 < PER:
-                nxt = scores(r + 1)
-            hd = g * PER + r
-            s = jnp.where(band, s, NEG)
-            top = jnp.max(s, axis=1, keepdims=True)
-            p = jnp.exp2(s * EXP2_SCALE - top * EXP2_SCALE).astype(bf16)
-            o = dot(p, vv, 1, 0)
-            comb[:, hd * D : (hd + 1) * D] += o[:, :D] / o[:, D:]
-
-    window_group(0)
-    fenwick(1)
+    for kv in range(2):
+        @pl.when(yh == 0)
+        def _():
+            y_copy(kv, 2).start()
     z_start(1)
-    window_group(1)
-    fenwick(2)
+    z_forward(0)
+    w_start()
+
     b_start(0)
-    window_group(2)
-    fenwick(3)
-    z_start(2)
-    window_group(3)
-    fenwick(4)
-    z_start(3)
-    b_start(1)
-
-    for level in range(5):
-        scale = jnp.where((c // 2**level) % 2 == 1, (D * TOK * 2**level) ** -0.5, 0.0)
-        for g in range(GROUPS):
-            bucket = fr[level, g]
-            for r in range(PER):
-                hd = g * PER + r
-                term = dot(ql[:, hd * D : (hd + 1) * D], bucket, 1, 0)
-                at = hd * LEVELS + level + 1
-                comb[:, hd * D : (hd + 1) * D] += (lw[:, at : at + 1] * scale) * term
 
     acc[...] = jnp.zeros_like(acc)
     mx[...] = jnp.full_like(mx, NEG)
@@ -297,30 +278,27 @@
     def r_copy(blk):
         return remote(
             ob.at[blk], cr.at[x], rs.at[blk], rr.at[x],
-            blk * 8 + flip(blk) * 2 + core, role_head,
+            blk * 8 + z * 2 + core, role_head,
         )
+
+    place = z * 2 + core
 
     def chunk_step(chunk, carry):
         b_wait(chunk)
 
-        @pl.when(chunk < 3)
-        def _():
-            @pl.when(chunk > 0)
-            def _():
-                b_start(chunk + 1)
-
-        place = flip(chunk) * 2 + core
-
-        def full_half(part, carry2):
-            attend(chunk, half_kv(kb, chunk, part), half_kv(vb, chunk, part), None)
-            return carry2
-
-        lax.fori_loop(0, place // 4, full_half, 0)
-        part = place // 4
-        first = (place % 4) * TOK
-        row = lax.broadcasted_iota(jnp.int32, (TOK, half), 0) + first
-        col = lax.broadcasted_iota(jnp.int32, (TOK, half), 1)
-        attend(chunk, half_kv(kb, chunk, part), half_kv(vb, chunk, part), col <= row)
+        def masked(size, kk, vv):
+            row = lax.broadcasted_iota(jnp.int32, (TOK, size), 0) + place * TOK
+            col = lax.broadcasted_iota(jnp.int32, (TOK, size), 1)
+            attend(chunk, kk, vv, col <= row)
+
+        @pl.when(z < 2)
+        def _():
+            masked(half, half_kv(kb, chunk, 0), half_kv(vb, chunk, 0))
+
+        @pl.when(z >= 2)
+        def _():
+            masked(2048, kb[chunk].reshape(2048, D), vb[chunk].reshape(2048, D))
+
         for r in range(PER):
             sl = pl.ds(r * TOK, TOK)
             ob[chunk, :, r * D : (r + 1) * D] = (
@@ -336,7 +314,39 @@
         def _():
             r_copy(chunk).start()
 
+        @pl.when(chunk == 0)
+        def _():
+            fenwick(0)
+            z_start(2)
+            z_forward(1)
+
+        @pl.when(chunk == 1)
+        def _():
+            b_start(2)
+            fenwick(4)
+
+        @pl.when(chunk == 2)
+        def _():
+            b_start(3)
+
         def full(blk, carry2):
+            @pl.when((chunk == 0) & (blk == 1))
+            def _():
+                fenwick(1)
+                z_start(3)
+                b_start(1)
+
+            @pl.when((chunk == 0) & (blk == 2))
+            def _():
+                fenwick(2)
+                z_forward(2)
+
+            @pl.when((chunk == 0) & (blk == 3))
+            def _():
+                fenwick(3)
+                z_forward(3)
+                w_arrive()
+
             attend(blk, kb[chunk].reshape(2048, D), vb[chunk].reshape(2048, D), None)
             return carry2
 
@@ -344,6 +354,49 @@
         return carry
 
     lax.fori_loop(0, 4, chunk_step, 0)
+
+    for level in range(5):
+        scale = jnp.where((c // 2**level) % 2 == 1, (D * TOK * 2**level) ** -0.5, 0.0)
+        for g in range(GROUPS):
+            bucket = fr[level, g]
+            for r in range(PER):
+                hd = g * PER + r
+                term = dot(ql[:, hd * D : (hd + 1) * D], bucket, 1, 0)
+                at = hd * LEVELS + level + 1
+                comb[:, hd * D : (hd + 1) * D] += (lw[:, at : at + 1] * scale) * term
+
+    for kv in range(2):
+        y_copy(kv, 0).wait_recv()
+
+    far = 3 * TOK
+    row = lax.broadcasted_iota(jnp.int32, (TOK, far), 0) + 2 * TOK
+    col = lax.broadcasted_iota(jnp.int32, (TOK, far), 1)
+    band = (col <= row) & (col > row - W) & (col >= (2 - c) * TOK)
+    ones = jnp.ones((far, D), bf16)
+
+    def window_group(g):
+        kk = wk[:, :, g * D : (g + 1) * D].reshape(far, D)
+        vv = jnp.concatenate([wv[:, :, g * D : (g + 1) * D].reshape(far, D), ones], axis=1)
+
+        def scores(r):
+            hd = g * PER + r
+            return dot(qw[:, hd * D : (hd + 1) * D], kk, 1, 1)
+
+        nxt = scores(0)
+        for r in range(PER):
+            s = nxt
+            if r + 1 < PER:
+                nxt = scores(r + 1)
+            hd = g * PER + r
+            s = jnp.where(band, s, NEG)
+            top = jnp.max(s, axis=1, keepdims=True)
+            p = jnp.exp2(s * EXP2_SCALE - top * EXP2_SCALE).astype(bf16)
+            o = dot(p, vv, 1, 0)
+            comb[:, hd * D : (hd + 1) * D] += o[:, :D] / o[:, D:]
+
+    for g in range(GROUPS):
+        window_group(g)
+
 
     square = jnp.zeros((TOK, D), f32)
     for j in range(4):
@@ -380,16 +433,14 @@
             r_copy(j).wait_send()
         for kv in range(2):
             b_copy(kv, j).wait_send()
-            for dz in range(1, 4):
-                z_copy(kv, j, dz).wait_send()
-    for o in (1, 2):
-        for kv in range(2):
-            @pl.when(c + o < CTX)
-            def _():
-                remote(
-                    (k_win, v_win)[kv], (wk, wv)[kv].at[2 - o],
-                    ws.at[kv, o - 1], wr.at[kv, o - 1], c, h,
-                ).wait_send()
+            for step in range(3):
+                z_copy(kv, j, step).wait_send()
+    for kv in range(2):
+        y_copy(kv, 0).wait_send()
+
+        @pl.when(c + 2 < CTX)
+        def _():
+            w_copy(kv).wait_send()
     for level in range(5):
         f_copy(level).wait_send()
     for d in range(1, 4):

time: 131 us -> 97.5 us (0.74)
  the two profiles are of different devices: /device:TPU:7 before, /device:TPU:71 now
where the time goes in v1:
time: 97.5 us; the launch traced here: 97.3 us
  Pallas kernels  93.4 us (96%)
  local copies, waits for them, and re-layouts  3.83 us (4%)
    pallas_call x1, Pallas kernels, per_device(): pl.pallas_call(kernel, out_shape=jax.ShapeDtypeStruct((TOK, HEADS * D), b...  93.4 us
    unnamed x2, local copies, waits for them, and re-layouts  3.12 us

profile of v1, /device:TPU:71, one launch (start us, length us, event | category | flops | bytes accessed | tf_op | source)
XLA Modules:
  0.0 97.3 jit_solution(13556003256040887735)
XLA Ops:
  0.0 0.8 copy.14
  0.8 0.7 copy.15.table
  1.5 93.4 %hybrid_attention.1 = bf16[256,2048]{1,0:T(8,128)(2,1)} custom-call(bf16[256,2048]{1,0:T(8,128)(2,1)} %q_win.1, bf16[256,512]{1,0:T(8,128)(2,1)} %k_win.1, bf16[256,512]{1,0:T(8,128)(2,1)} %v_win.1, bf16[256,2048]{1,0:T(8,128)(2,1)} %q_lin.1, bf16[256,512]{1,0:T(8,128)(2,1)} %k_lin.1, bf16[256,512]{1,0:T(8,128)(2,1)} %v_lin.1, f32[64,96]{1,0:T(8,128)} %copy.15.table, ...), custom_call_target="tpu_custom_call" | custom-call | tf_op jit(solution)/shard_map/hybrid_attention/pallas_call | solution.py:459
  94.9 2.3 %copy.17 = bf16[256,2048]{1,0:T(8,128)(2,1)} copy(bf16[256,2048]{1,0:T(8,128)(2,1)} %hybrid_attention.1) | data formatting | bytes 2097152
  (1 shorter events, 0.0 us)

commit v2 on v1

--- a/solution.py
+++ b/solution.py
@@ -117,23 +117,8 @@
 
     def s1_copy(j, kv):
         src = (k_sh, v_sh)[kv].at[:, pl.ds(j * D, D)]
-        dst = (kb, vb)[kv].at[x, z, pl.ds(yh * TOK, TOK), :]
+        dst = (kb, vb)[kv].at[z, x, pl.ds(yh * TOK, TOK), :]
         return src, dst
-
-    for j in range(4):
-        for kv in range(2):
-            src, dst = s1_copy(j, kv)
-            local = mixed & (x == j)
-
-            @pl.when(local)
-            def _():
-                pltpu.make_async_copy(src, dst, s1r.at[kv, j]).start()
-
-            @pl.when(jnp.logical_not(local))
-            def _():
-                remote(
-                    src, dst, s1s.at[kv, j], s1r.at[kv, x], j * 8 + z * 2 + core, role_head
-                ).start()
 
     def f_copy(level):
         return remote(
@@ -152,52 +137,79 @@
     f_copy(0).start()
 
     for j in range(4):
-        src = q_cross.at[:, pl.ds(j * GC, GC)]
-        dst = qb.at[x]
-        local = mixed & (x == j)
-
-        @pl.when(local)
-        def _():
-            pltpu.make_async_copy(src, dst, qr.at[j]).start()
-
-        @pl.when(jnp.logical_not(local))
-        def _():
-            remote(src, dst, qs.at[j], qr.at[x], j * 8 + z * 2 + core, role_head).start()
-
-    def z_copy(kv, chunk, step):
-        tile = (z + 1) % 4 if step == 2 else z
-        to = (z + 1) % 4 if step == 0 else (z + 3) % 4
-        part = (kb, vb)[kv].at[chunk, tile, pl.ds(core * TOK, TOK), :]
+        for kv in range(2):
+            src, dst = s1_copy(j, kv)
+            local = mixed & (x == j)
+
+            @pl.when(local)
+            def _():
+                pltpu.make_async_copy(src, dst, s1r.at[kv, j]).start()
+
+            @pl.when(jnp.logical_not(local))
+            def _():
+                remote(
+                    src, dst, s1s.at[kv, j], s1r.at[kv, x], j * 8 + z * 2 + core, role_head
+                ).start()
+
+    def q_copy(t):
+        j = (x + 4 - t) % 4
+        return (
+            q_cross.at[:, pl.ds(j * GC, GC)], qb.at[x], qs.at[t], qr.at[x],
+            j * 8 + z * 2 + core, role_head,
+        )
+
+    def q_start(t):
+        src, dst, ssem, rsem, cc, hh = q_copy(t)
+        if t == 0:
+            @pl.when(mixed)
+            def _():
+                pltpu.make_async_copy(src, dst, rsem).start()
+
+            @pl.when(jnp.logical_not(mixed))
+            def _():
+                remote(src, dst, ssem, rsem, cc, hh).start()
+        else:
+            remote(src, dst, ssem, rsem, cc, hh).start()
+
+    def z_copy(kv, step):
+        if step == 2:
+            tile, to = ((z + 1) % 4, (z + 3) % 4) if kv == 0 else ((z + 3) % 4, (z + 1) % 4)
+        else:
+            tile, to = z, (z + 1 + 2 * step) % 4
+        part = (kb, vb)[kv].at[tile, :, pl.ds(core * TOK, TOK), :]
         return remote(
-            part, part, zs.at[kv, chunk, step], zr.at[kv, chunk, step],
-            x * 8 + to * 2 + yh, h,
-        )
-
-    def z_start(chunk):
-        for kv in range(2):
-            part = (kb, vb)[kv].at[chunk, z, pl.ds(core * TOK, TOK), :]
-            remote(part, part, s1s.at[kv, 0], s1r.at[kv, chunk], c, h).wait_recv()
-            for step in (1, 0):
-                z_copy(kv, chunk, step).start()
-
-    def z_forward(chunk):
-        for kv in range(2):
-            z_copy(kv, chunk, 1).wait_recv()
-            z_copy(kv, chunk, 2).start()
-
-    def b_copy(kv, chunk):
-        part = (kb, vb)[kv].at[chunk, :, pl.ds(core * TOK, TOK), :]
-        return remote(part, part, bs.at[kv, chunk], br.at[kv, chunk], c, h + 1 - 2 * core)
-
-    def b_start(chunk):
-        for kv in range(2):
-            for step in (0, 2):
-                z_copy(kv, chunk, step).wait_recv()
-            b_copy(kv, chunk).start()
-
-    def b_wait(chunk):
-        for kv in range(2):
-            b_copy(kv, chunk).wait_recv()
+            part, part, zs.at[kv, step], zr.at[kv, step], x * 8 + to * 2 + yh, h
+        )
+
+    def z_of(n):
+        return (z + jnp.where(n == 1, 3, jnp.where(n == 2, 1, jnp.where(n == 3, 2, 0)))) % 4
+
+    def b_copy(kv, n):
+        part = (kb, vb)[kv].at[z_of(n), :, pl.ds(core * TOK, TOK), :]
+        return remote(part, part, bs.at[kv, n], br.at[kv, n], c, h + 1 - 2 * core)
+
+    def b_start(n):
+        for kv in range(2):
+            if n > 0:
+                z_copy(kv, n - 1).wait_recv()
+            b_copy(kv, n).start()
+        if n == 1:
+            z_copy(1, 2).start()
+        if n == 2:
+            z_copy(0, 2).start()
+
+    def b_wait(n):
+        for kv in range(2):
+            b_copy(kv, n).wait_recv()
+
+    def own_chunk():
+        for kv in range(2):
+            for j in range(4):
+                part = (kb, vb)[kv].at[z, j, pl.ds(core * TOK, TOK), :]
+                remote(part, part, s1s.at[kv, 0], s1r.at[kv, j], c, h).wait_recv()
+            for step in (0, 1):
+                z_copy(kv, step).start()
+        b_start(0)
 
     def w_copy(kv):
         return remote(
@@ -230,26 +242,23 @@
             def _():
                 y_copy(kv, 0).start()
 
-    z_start(0)
+    w_start()
+    q_start(0)
+    own_chunk()
+    for t in range(1, 4):
+        q_start(t)
+    fenwick(0)
     for i in (3, 4, 5):
         loads[i].wait()
-    for kv in range(2):
-        @pl.when(yh == 0)
-        def _():
-            y_copy(kv, 2).start()
-    z_start(1)
-    z_forward(0)
-    w_start()
-
-    b_start(0)
-
-    acc[...] = jnp.zeros_like(acc)
-    mx[...] = jnp.full_like(mx, NEG)
-    for j in range(4):
-        remote(q_cross.at[:, pl.ds(0, GC)], qb.at[j], qs.at[j], qr.at[j], c, h).wait_recv()
-
-    def attend(blk, kk, vv, mask):
-        size = kk.shape[0]
+
+    step_row = lax.broadcasted_iota(jnp.int32, (TOK, 2 * TOK), 0) + core * TOK
+    step_col = lax.broadcasted_iota(jnp.int32, (TOK, 2 * TOK), 1)
+    step_mask = step_col <= step_row
+
+    def attend(blk, chunk, parts, first):
+        size = parts * 2 * TOK
+        kk = kb[chunk, :parts].reshape(size, D)
+        vv = vb[chunk, :parts].reshape(size, D)
         vv = jnp.concatenate([vv, jnp.ones((size, D), bf16)], axis=1)
 
         def scores(r):
@@ -260,20 +269,20 @@
             s = nxt
             if r + 1 < PER:
                 nxt = scores(r + 1)
-            if mask is not None:
-                s = jnp.where(mask, s, NEG)
             sl = pl.ds(r * TOK, TOK)
-            old = mx[blk, sl, :][:, :1]
-            new = jnp.maximum(old, jnp.max(s, axis=1, keepdims=True))
+            if first:
+                last = jnp.where(step_mask, s[:, size - 2 * TOK :], NEG)
+                s = last if parts == 1 else jnp.concatenate([s[:, : size - 2 * TOK], last], axis=1)
+                new = jnp.max(s, axis=1, keepdims=True)
+            else:
+                old = mx[blk, sl, :][:, :1]
+                new = jnp.maximum(old, jnp.max(s, axis=1, keepdims=True))
             p = jnp.exp2(s * EXP2_SCALE - new * EXP2_SCALE).astype(bf16)
-            damp = jnp.exp2((old - new) * EXP2_SCALE)
-            acc[blk, sl, :] = acc[blk, sl, :] * damp + dot(p, vv, 1, 0)
+            o = dot(p, vv, 1, 0)
+            if not first:
+                o += acc[blk, sl, :] * jnp.exp2((old - new) * EXP2_SCALE)
+            acc[blk, sl, :] = o
             mx[blk, sl, :] = jnp.broadcast_to(new, (TOK, D))
-
-    half = 1024
-
-    def half_kv(ref, chunk, part):
-        return ref[chunk, pl.ds(part * 2, 2)].reshape(half, D)
 
     def r_copy(blk):
         return remote(
@@ -281,79 +290,73 @@
             blk * 8 + z * 2 + core, role_head,
         )
 
-    place = z * 2 + core
-
-    def chunk_step(chunk, carry):
-        b_wait(chunk)
-
-        def masked(size, kk, vv):
-            row = lax.broadcasted_iota(jnp.int32, (TOK, size), 0) + place * TOK
-            col = lax.broadcasted_iota(jnp.int32, (TOK, size), 1)
-            attend(chunk, kk, vv, col <= row)
-
-        @pl.when(z < 2)
-        def _():
-            masked(half, half_kv(kb, chunk, 0), half_kv(vb, chunk, 0))
-
-        @pl.when(z >= 2)
-        def _():
-            masked(2048, kb[chunk].reshape(2048, D), vb[chunk].reshape(2048, D))
-
+    def send_back(blk):
         for r in range(PER):
             sl = pl.ds(r * TOK, TOK)
-            ob[chunk, :, r * D : (r + 1) * D] = (
-                acc[chunk, sl, :D] / acc[chunk, sl, D:]
-            ).astype(bf16)
-        local = mixed & (x == chunk)
+            ob[blk, :, r * D : (r + 1) * D] = (acc[blk, sl, :D] / acc[blk, sl, D:]).astype(bf16)
+        local = mixed & (x == blk)
 
         @pl.when(local)
         def _():
-            pltpu.make_async_copy(ob.at[chunk], cr.at[x], rr.at[x]).start()
+            pltpu.make_async_copy(ob.at[blk], cr.at[x], rr.at[x]).start()
 
         @pl.when(jnp.logical_not(local))
         def _():
-            r_copy(chunk).start()
-
-        @pl.when(chunk == 0)
-        def _():
-            fenwick(0)
-            z_start(2)
-            z_forward(1)
-
-        @pl.when(chunk == 1)
-        def _():
-            b_start(2)
-            fenwick(4)
-
-        @pl.when(chunk == 2)
-        def _():
-            b_start(3)
-
-        def full(blk, carry2):
-            @pl.when((chunk == 0) & (blk == 1))
-            def _():
-                fenwick(1)
-                z_start(3)
-                b_start(1)
-
-            @pl.when((chunk == 0) & (blk == 2))
-            def _():
-                fenwick(2)
-                z_forward(2)
-
-            @pl.when((chunk == 0) & (blk == 3))
-            def _():
-                fenwick(3)
-                z_forward(3)
-                w_arrive()
-
-            attend(blk, kb[chunk].reshape(2048, D), vb[chunk].reshape(2048, D), None)
-            return carry2
-
-        lax.fori_loop(chunk + 1, 4, full, 0)
+            r_copy(blk).start()
+
+    def w_y_start():
+        for kv in range(2):
+            @pl.when(yh == 0)
+            def _():
+                y_copy(kv, 2).start()
+
+    events = {
+        0: [lambda: b_wait(0)],
+        1: [lambda: fenwick(1)],
+        2: [w_y_start],
+        3: [lambda: fenwick(2), w_arrive],
+        4: [lambda: b_start(1), lambda: b_start(2), lambda: b_wait(1)],
+        6: [lambda: fenwick(3)],
+        8: [lambda: b_wait(2)],
+        10: [lambda: fenwick(4), lambda: b_start(3)],
+        12: [lambda: b_wait(3)],
+    }
+
+    def step(i, carry):
+        n = i // 4
+        chunk = z_of(n)
+        blk = (x + i + jnp.where(n == 3, 1, 0)) % 4
+        for at, todo in events.items():
+            @pl.when(i == at)
+            def _():
+                for do in todo:
+                    do()
+
+        @pl.when(n == 0)
+        def _():
+            remote(
+                q_cross.at[:, pl.ds(0, GC)], qb.at[blk], qs.at[0], qr.at[blk], c, h
+            ).wait_recv()
+            for j in range(4):
+                @pl.when(blk == j)
+                def _():
+                    attend(blk, chunk, j + 1, True)
+
+        @pl.when(n > 0)
+        def _():
+            parts = blk + jnp.where(chunk < z, 1, 0)
+            for j in range(1, 5):
+                @pl.when(parts == j)
+                def _():
+                    attend(blk, chunk, j, False)
+
+        @pl.when(n == 3)
+        def _():
+            send_back(blk)
+
         return carry
 
-    lax.fori_loop(0, 4, chunk_step, 0)
+    lax.fori_loop(0, 16, step, 0)
 
     for level in range(5):
         scale = jnp.where((c // 2**level) % 2 == 1, (D * TOK * 2**level) ** -0.5, 0.0)
@@ -427,14 +430,19 @@
             for kv in range(2):
                 src, dst = s1_copy(j, kv)
                 remote(src, dst, s1s.at[kv, j], s1r.at[kv, x], c, h).wait_send()
-            remote(
-                q_cross.at[:, pl.ds(j * GC, GC)], qb.at[x], qs.at[j], qr.at[x], c, h
-            ).wait_send()
             r_copy(j).wait_send()
         for kv in range(2):
             b_copy(kv, j).wait_send()
-            for step in range(3):
-                z_copy(kv, j, step).wait_send()
+    for kv in range(2):
+        for n in range(3):
+            z_copy(kv, n).wait_send()
+
+    @pl.when(jnp.logical_not(mixed))
+    def _():
+        remote(*q_copy(0)).wait_send()
+
+    for t in range(1, 4):
+        remote(*q_copy(t)).wait_send()
     for kv in range(2):
         y_copy(kv, 0).wait_send()
 
@@ -487,7 +495,7 @@
             dma((2, 2)), dma((2, 2)),
             dma((4,)), dma((4,)),
             dma((5,)), dma((5,)),
-            dma((2, 4, 3)), dma((2, 4, 3)),
+            dma((2, 3)), dma((2, 3)),
             dma((2, 4)), dma((2, 4)),
             dma((4,)), dma((4,)),
             dma((3,)), dma((3,)),

time: 97.5 us -> 89.6 us (0.919)
  the two profiles are of different devices: /device:TPU:71 before, /device:TPU:97 now
where the time goes in v2:
time: 89.6 us; the launch traced here: 88.2 us
  Pallas kernels  84.3 us (94%)
  local copies, waits for them, and re-layouts  3.83 us (4%)
    pallas_call x1, Pallas kernels, per_device(): pl.pallas_call(kernel, out_shape=jax.ShapeDtypeStruct((TOK, HEADS * D), b...  84.3 us
    unnamed x2, local copies, waits for them, and re-layouts  3.12 us

profile of v2, /device:TPU:97, one launch (start us, length us, event | category | flops | bytes accessed | tf_op | source)
XLA Modules:
  0.0 88.2 jit_solution(6965397407460276679)
XLA Ops:
  0.0 0.8 copy.14
  0.8 0.7 copy.15.table
  1.5 84.3 %hybrid_attention.1 = bf16[256,2048]{1,0:T(8,128)(2,1)} custom-call(bf16[256,2048]{1,0:T(8,128)(2,1)} %q_win.1, bf16[256,512]{1,0:T(8,128)(2,1)} %k_win.1, bf16[256,512]{1,0:T(8,128)(2,1)} %v_win.1, bf16[256,2048]{1,0:T(8,128)(2,1)} %q_lin.1, bf16[256,512]{1,0:T(8,128)(2,1)} %k_lin.1, bf16[256,512]{1,0:T(8,128)(2,1)} %v_lin.1, f32[64,96]{1,0:T(8,128)} %copy.15.table, ...), custom_call_target="tpu_custom_call" | custom-call | tf_op jit(solution)/shard_map/hybrid_attention/pallas_call | solution.py:467
  85.9 2.3 %copy.17 = bf16[256,2048]{1,0:T(8,128)(2,1)} copy(bf16[256,2048]{1,0:T(8,128)(2,1)} %hybrid_attention.1) | data formatting | bytes 2097152
  (1 shorter events, 0.0 us)

commit v3 on v2

--- a/solution.py
+++ b/solution.py
@@ -28,10 +28,10 @@
 
 def kernel(
     q_win, k_win, v_win, q_lin, k_lin, v_lin, table, index, q_cross, k_sh, v_sh, gain,
-    out,
-    ql, kl, vl, qw, wk, wv, qb, kb, vb, ob, cr, acc, mx, comb, lw,
+    comb, norm,
+    ql, kl, vl, qw, wk, wv, qb, kb, vb, ob, cr, acc, mx, lw,
     state, fs, fr, hs, hr,
-    in_sem, s1s, s1r, ws, wr, qs, qr, fss, frs, zs, zr, bs, br, rs, rr, hss, hrs,
+    in_sem, s1s, s1r, ws, wr, qs, qr, fss, frs, zs, zr, fs2, fr2, bs, br, rs, rr, hss, hrs,
 ):
     c = lax.axis_index("ctx")
     h = lax.axis_index("head")
@@ -93,6 +93,144 @@
         own = dot(kl[:, g * D : (g + 1) * D], vl[:, g * D : (g + 1) * D], 0, 0)
         state[g] = own
         fs[0, g] = own.astype(bf16)
+
+    pl.semaphore_wait(
+        barrier,
+        jnp.where(mixed, 3, 6) + 7 + jnp.where((z == 0) | (z == 3), 1, 0),
+    )
+
+    def s1_copy(j, kv):
+        src = (k_sh, v_sh)[kv].at[:, pl.ds(j * D, D)]
+        dst = (kb, vb)[kv].at[z, x, pl.ds(yh * TOK, TOK), :]
+        return src, dst
+
+    def f_copy(level):
+        return remote(
+            fs.at[level], fr.at[level], fss.at[level], frs.at[level], partner(level), h
+        )
+
+    def fenwick(level):
+        f_copy(level).wait_recv()
+        got = fr[level]
+        if level < 4:
+            total = state[...] + got.astype(f32)
+            state[...] = total
+            fs[level + 1] = total.astype(bf16)
+            f_copy(level + 1).start()
+
+    for j in range(4):
+        for kv in range(2):
+            src, dst = s1_copy(j, kv)
+            local = mixed & (x == j)
+
+            @pl.when(local)
+            def _():
+                pltpu.make_async_copy(src, dst, s1r.at[kv, j]).start()
+
+            @pl.when(jnp.logical_not(local))
+            def _():
+                remote(
+                    src, dst, s1s.at[kv, j], s1r.at[kv, x], j * 8 + z * 2 + core, role_head
+                ).start()
+
+    def q_copy(t):
+        j = (x + 4 - t) % 4
+        return (
+            q_cross.at[:, pl.ds(j * GC, GC)], qb.at[x], qs.at[t], qr.at[x],
+            j * 8 + z * 2 + core, role_head,
+        )
+
+    def q_start(t):
+        src, dst, ssem, rsem, cc, hh = q_copy(t)
+        if t == 0:
+            @pl.when(mixed)
+            def _():
+                pltpu.make_async_copy(src, dst, rsem).start()
+
+            @pl.when(jnp.logical_not(mixed))
+            def _():
+                remote(src, dst, ssem, rsem, cc, hh).start()
+        else:
+            remote(src, dst, ssem, rsem, cc, hh).start()
+
+    def z_copy(kv, step, j):
+        part = (kb, vb)[kv].at[z, j, pl.ds(core * TOK, TOK), :]
+        return remote(
+            part, part, zs.at[kv, step, j], zr.at[kv, step, j],
+            x * 8 + (z + 1 + 2 * step) % 4 * 2 + yh, h,
+        )
+
+    def z_forward(kv):
+        tile, to = ((z + 1) % 4, (z + 3) % 4) if kv == 0 else ((z + 3) % 4, (z + 1) % 4)
+        part = (kb, vb)[kv].at[tile, :, pl.ds(core * TOK, TOK), :]
+        return remote(part, part, fs2.at[kv], fr2.at[kv], x * 8 + to * 2 + yh, h)
+
+    def z_of(n):
+        return (z + jnp.where(n == 1, 3, jnp.where(n == 2, 1, jnp.where(n == 3, 2, 0)))) % 4
+
+    def b_copy(kv, n):
+        part = (kb, vb)[kv].at[z_of(n), :, pl.ds(core * TOK, TOK), :]
+        return remote(part, part, bs.at[kv, n], br.at[kv, n], c, h + 1 - 2 * core)
+
+    def b_start(n):
+        for kv in range(2):
+            if n == 3:
+                z_forward(kv).wait_recv()
+            elif n > 0:
+                for j in range(4):
+                    z_copy(kv, n - 1, j).wait_recv()
+            b_copy(kv, n).start()
+        if n == 1:
+            z_forward(1).start()
+        if n == 2:
+            z_forward(0).start()
+
+    def b_wait(n):
+        for kv in range(2):
+            b_copy(kv, n).wait_recv()
+
+    def own_chunk():
+        for d in (0, 1, 3, 2):
+            j = (x + d) % 4
+            for kv in range(2):
+                part = (kb, vb)[kv].at[z, j, pl.ds(core * TOK, TOK), :]
+                remote(part, part, s1s.at[kv, 0], s1r.at[kv, j], c, h).wait_recv()
+                for step in (0, 1):
+                    z_copy(kv, step, j).start()
+        b_start(0)
+
+    def w_copy(kv):
+        return remote(
+            (k_win, v_win)[kv], (wk, wv)[kv].at[0], ws.at[kv, 0], wr.at[kv, 0], c + 2, h
+        )
+
+    def w_start():
+        for kv in range(2):
+            @pl.when(c + 2 < CTX)
+            def _():
+                w_copy(kv).start()
+
+    def y_copy(kv, slot):
+        ref = (wk, wv)[kv]
+        return remote(ref.at[slot], ref.at[1], ws.at[kv, 1], wr.at[kv, 1], partner(0), h)
+
+    def w_arrive():
+        for kv in range(2):
+            ref = (wk, wv)[kv]
+
+            @pl.when(c >= 2)
+            def _():
+                w_copy(kv).wait_recv()
+
+            @pl.when(c < 2)
+            def _():
+                ref[0] = jnp.zeros((TOK, GROUPS * D), bf16)
+
+            @pl.when(yh == 1)
+            def _():
+                y_copy(kv, 0).start()
+
+    w_start()
 
     hot = (lax.broadcasted_iota(jnp.int32, (64, TOK), 0) == index[...]).astype(f32)
     lw[...] = dot(hot, table[...], 0, 0, lax.Precision.HIGHEST)
@@ -110,144 +248,10 @@
                 s, vl[:, g * D : (g + 1) * D], 1, 0
             )
 
-    pl.semaphore_wait(
-        barrier,
-        jnp.where(mixed, 3, 6) + 7 + jnp.where((z == 0) | (z == 3), 1, 0),
-    )
-
-    def s1_copy(j, kv):
-        src = (k_sh, v_sh)[kv].at[:, pl.ds(j * D, D)]
-        dst = (kb, vb)[kv].at[z, x, pl.ds(yh * TOK, TOK), :]
-        return src, dst
-
-    def f_copy(level):
-        return remote(
-            fs.at[level], fr.at[level], fss.at[level], frs.at[level], partner(level), h
-        )
-
-    def fenwick(level):
-        f_copy(level).wait_recv()
-        got = fr[level]
-        if level < 4:
-            total = state[...] + got.astype(f32)
-            state[...] = total
-            fs[level + 1] = total.astype(bf16)
-            f_copy(level + 1).start()
-
+    own_chunk()
+    for t in range(4):
+        q_start(t)
     f_copy(0).start()
-
-    for j in range(4):
-        for kv in range(2):
-            src, dst = s1_copy(j, kv)
-            local = mixed & (x == j)
-
-            @pl.when(local)
-            def _():
-                pltpu.make_async_copy(src, dst, s1r.at[kv, j]).start()
-
-            @pl.when(jnp.logical_not(local))
-            def _():
-                remote(
-                    src, dst, s1s.at[kv, j], s1r.at[kv, x], j * 8 + z * 2 + core, role_head
-                ).start()
-
-    def q_copy(t):
-        j = (x + 4 - t) % 4
-        return (
-            q_cross.at[:, pl.ds(j * GC, GC)], qb.at[x], qs.at[t], qr.at[x],
-            j * 8 + z * 2 + core, role_head,
-        )
-
-    def q_start(t):
-        src, dst, ssem, rsem, cc, hh = q_copy(t)
-        if t == 0:
-            @pl.when(mixed)
-            def _():
-                pltpu.make_async_copy(src, dst, rsem).start()
-
-            @pl.when(jnp.logical_not(mixed))
-            def _():
-                remote(src, dst, ssem, rsem, cc, hh).start()
-        else:
-            remote(src, dst, ssem, rsem, cc, hh).start()
-
-    def z_copy(kv, step):
-        if step == 2:
-            tile, to = ((z + 1) % 4, (z + 3) % 4) if kv == 0 else ((z + 3) % 4, (z + 1) % 4)
-        else:
-            tile, to = z, (z + 1 + 2 * step) % 4
-        part = (kb, vb)[kv].at[tile, :, pl.ds(core * TOK, TOK), :]
-        return remote(
-            part, part, zs.at[kv, step], zr.at[kv, step], x * 8 + to * 2 + yh, h
-        )
-
-    def z_of(n):
-        return (z + jnp.where(n == 1, 3, jnp.where(n == 2, 1, jnp.where(n == 3, 2, 0)))) % 4
-
-    def b_copy(kv, n):
-        part = (kb, vb)[kv].at[z_of(n), :, pl.ds(core * TOK, TOK), :]
-        return remote(part, part, bs.at[kv, n], br.at[kv, n], c, h + 1 - 2 * core)
-
-    def b_start(n):
-        for kv in range(2):
-            if n > 0:
-                z_copy(kv, n - 1).wait_recv()
-            b_copy(kv, n).start()
-        if n == 1:
-            z_copy(1, 2).start()
-        if n == 2:
-            z_copy(0, 2).start()
-
-    def b_wait(n):
-        for kv in range(2):
-            b_copy(kv, n).wait_recv()
-
-    def own_chunk():
-        for kv in range(2):
-            for j in range(4):
-                part = (kb, vb)[kv].at[z, j, pl.ds(core * TOK, TOK), :]
-                remote(part, part, s1s.at[kv, 0], s1r.at[kv, j], c, h).wait_recv()
-            for step in (0, 1):
-                z_copy(kv, step).start()
-        b_start(0)
-
-    def w_copy(kv):
-        return remote(
-            (k_win, v_win)[kv], (wk, wv)[kv].at[0], ws.at[kv, 0], wr.at[kv, 0], c + 2, h
-        )
-
-    def w_start():
-        for kv in range(2):
-            @pl.when(c + 2 < CTX)
-            def _():
-                w_copy(kv).start()
-
-    def y_copy(kv, slot):
-        ref = (wk, wv)[kv]
-        return remote(ref.at[slot], ref.at[1], ws.at[kv, 1], wr.at[kv, 1], partner(0), h)
-
-    def w_arrive():
-        for kv in range(2):
-            ref = (wk, wv)[kv]
-
-            @pl.when(c >= 2)
-            def _():
-                w_copy(kv).wait_recv()
-
-            @pl.when(c < 2)
-            def _():
-                ref[0] = jnp.zeros((TOK, GROUPS * D), bf16)
-
-            @pl.when(yh == 1)
-            def _():
-                y_copy(kv, 0).start()
-
-    w_start()
-    q_start(0)
-    own_chunk()
-    for t in range(1, 4):
-        q_start(t)
-    fenwick(0)
     for i in (3, 4, 5):
         loads[i].wait()
 
@@ -312,14 +316,15 @@
 
     events = {
         0: [lambda: b_wait(0)],
-        1: [lambda: fenwick(1)],
         2: [w_y_start],
-        3: [lambda: fenwick(2), w_arrive],
+        3: [lambda: fenwick(0), w_arrive],
         4: [lambda: b_start(1), lambda: b_start(2), lambda: b_wait(1)],
-        6: [lambda: fenwick(3)],
+        5: [lambda: fenwick(1)],
+        7: [lambda: fenwick(2)],
         8: [lambda: b_wait(2)],
-        10: [lambda: fenwick(4), lambda: b_start(3)],
-        12: [lambda: b_wait(3)],
+        9: [lambda: fenwick(3)],
+        11: [lambda: b_start(3)],
+        12: [lambda: b_wait(3), lambda: fenwick(4)],
     }
 
     def step(i, carry):
@@ -417,10 +422,7 @@
     for d in range(1, 4):
         remote(hs, hr.at[d - 1], hss.at[d - 1], hrs.at[d - 1], c, (h + d) % 4).wait_recv()
         total = total + hr[d - 1]
-    norm = lax.rsqrt(total / (4 * HEADS * D) + 1e-6).T[:, :1]
-    for hd in range(HEADS):
-        at = slice(hd * D, (hd + 1) * D)
-        out[:, at] = (comb[:, at] * norm).astype(bf16)
+    norm[...] = lax.rsqrt(total / (4 * HEADS * D) + 1e-6).T
 
     for j in range(4):
         local = mixed & (x == j)
@@ -434,8 +436,10 @@
         for kv in range(2):
             b_copy(kv, j).wait_send()
     for kv in range(2):
-        for n in range(3):
-            z_copy(kv, n).wait_send()
+        z_forward(kv).wait_send()
+        for j in range(4):
+            for n in range(2):
+                z_copy(kv, n, j).wait_send()
 
     @pl.when(jnp.logical_not(mixed))
     def _():
@@ -464,11 +468,14 @@
     vmem = pl.BlockSpec(memory_space=pltpu.VMEM)
     smem = pl.BlockSpec(memory_space=pltpu.SMEM)
     kv = GROUPS * D
-    return pl.pallas_call(
+    comb, norm = pl.pallas_call(
         kernel,
-        out_shape=jax.ShapeDtypeStruct((TOK, HEADS * D), bf16),
+        out_shape=[
+            jax.ShapeDtypeStruct((TOK, HEADS * D), f32),
+            jax.ShapeDtypeStruct((TOK, 8), f32),
+        ],
         in_specs=[whole] * 6 + [vmem, vmem] + [whole] * 3 + [smem],
-        out_specs=vmem,
+        out_specs=[vmem, vmem],
         scratch_shapes=[
             pltpu.VMEM((TOK, HEADS * D), bf16),
             pltpu.VMEM((TOK, kv), bf16),
@@ -483,7 +490,6 @@
             pltpu.VMEM((4, TOK, GC), bf16),
             pltpu.VMEM((4, PER * TOK, 2 * D), f32),
             pltpu.VMEM((4, PER * TOK, D), f32),
-            pltpu.VMEM((TOK, HEADS * D), f32),
             pltpu.VMEM((TOK, HEADS * LEVELS), f32),
             pltpu.VMEM((GROUPS, D, D), f32),
             pltpu.VMEM((5, GROUPS, D, D), bf16),
@@ -495,7 +501,8 @@
             dma((2, 2)), dma((2, 2)),
             dma((4,)), dma((4,)),
             dma((5,)), dma((5,)),
-            dma((2, 3)), dma((2, 3)),
+            dma((2, 2, 4)), dma((2, 2, 4)),
+            dma((2,)), dma((2,)),
             dma((2, 4)), dma((2, 4)),
             dma((4,)), dma((4,)),
             dma((3,)), dma((3,)),
@@ -509,6 +516,7 @@
         level_table.reshape(level_table.shape[0], -1), level_index.reshape(1, -1),
         q_cross, k_shared, v_shared, head_gain,
     )
+    return (comb * norm[:, :1]).astype(bf16)
 
 
 def solution(mesh):

time: 89.6 us -> 92.5 us (1.032); the launches traced: 88.2 us -> 92.3 us
  other arithmetic: 0 us -> 2.75 us
  Pallas kernels: 84.3 us -> 87 us
  local copies, waits for them, and re-layouts: 3.83 us -> 2.53 us
    convert_element_type x0 -> x1, other arithmetic: none -> 2.75 us  [per_device(): return (comb * norm[:, :1]).astype(bf16)]
    pallas_call x1, Pallas kernels: 84.3 us -> 87 us  [per_device(): pl.pallas_call(kernel, out_shape=[jax.ShapeDtypeStruct((TOK, HEADS * D),...]
    unnamed x2 -> x1, local copies, waits for them, and re-layouts: 3.12 us -> 0.82 us
    slice x0 -> x1, local copies, waits for them, and re-layouts: none -> 1.01 us  [per_device(): return (comb * norm[:, :1]).astype(bf16)]
where the time goes in v3:
time: 92.5 us; the launch traced here: 92.3 us
  Pallas kernels  87 us (94%)
  other arithmetic  2.75 us (3%)
  local copies, waits for them, and re-layouts  2.53 us (3%)
    pallas_call x1, Pallas kernels, per_device(): pl.pallas_call(kernel, out_shape=[jax.ShapeDtypeStruct((TOK, HEADS * D),...  87 us
    convert_element_type x1, other arithmetic, per_device(): return (comb * norm[:, :1]).astype(bf16)  2.75 us

profile of v3, /device:TPU:97, one launch (start us, length us, event | category | flops | bytes accessed | tf_op | source)
XLA Modules:
  0.0 92.3 jit_solution(14652815502232454927)
XLA Ops:
  0.0 0.8 copy.14
  0.8 0.7 copy.15.table
  1.5 87.0 %hybrid_attention.1 = (f32[256,2048]{1,0:T(8,128)}, f32[256,8]{1,0:T(8,128)}) custom-call(bf16[256,2048]{1,0:T(8,128)(2,1)} %q_win.1, bf16[256,512]{1,0:T(8,128)(2,1)} %k_win.1, bf16[256,512]{1,0:T(8,128)(2,1)} %v_win.1, bf16[256,2048]{1,0:T(8,128)(2,1)} %q_lin.1, bf16[256,512]{1,0:T(8,128)(2,1)} %k_lin.1, bf16[256,512]{1,0:T(8,128)(2,1)} %v_lin.1, ...), custom_call_target="tpu_custom_call" | custom-call | tf_op jit(solution)/shard_map/hybrid_attention/pallas_call | solution.py:471
  88.5 1.0 %slice_reduce_fusion = f32[256]{0:T(256)S(1)} fusion(f32[256,8]{1,0:T(8,128)} %get-tuple-element.8), kind=kLoop, calls=%fused_computation.1 | loop fusion | bytes 2048 | tf_op jit(solution)/shard_map/slice | solution.py:519
  89.5 2.7 %multiply_convert_fusion = bf16[256,2048]{1,0:T(8,128)(2,1)} fusion(f32[256,2048]{1,0:T(8,128)} %get-tuple-element.7, f32[256]{0:T(256)S(1)} %slice_reduce_fusion), kind=kLoop, calls=%fused_computation | loop fusion | flops 1048576 | bytes 3146752 | tf_op jit(solution)/shard_map/convert_element_type | solution.py:519
  (1 shorter events, 0.0 us)

commit v4 on v2

--- a/solution.py
+++ b/solution.py
@@ -94,6 +94,139 @@
         state[g] = own
         fs[0, g] = own.astype(bf16)
 
+    pl.semaphore_wait(
+        barrier,
+        jnp.where(mixed, 3, 6) + 7 + jnp.where((z == 0) | (z == 3), 1, 0),
+    )
+
+    def s1_copy(j, kv):
+        src = (k_sh, v_sh)[kv].at[:, pl.ds(j * D, D)]
+        dst = (kb, vb)[kv].at[z, x, pl.ds(yh * TOK, TOK), :]
+        return src, dst
+
+    def f_copy(level):
+        return remote(
+            fs.at[level], fr.at[level], fss.at[level], frs.at[level], partner(level), h
+        )
+
+    def fenwick(level):
+        f_copy(level).wait_recv()
+        got = fr[level]
+        if level < 4:
+            total = state[...] + got.astype(f32)
+            state[...] = total
+            fs[level + 1] = total.astype(bf16)
+            f_copy(level + 1).start()
+
+    f_copy(0).start()
+
+    for j in range(4):
+        for kv in range(2):
+            src, dst = s1_copy(j, kv)
+            local = mixed & (x == j)
+
+            @pl.when(local)
+            def _():
+                pltpu.make_async_copy(src, dst, s1r.at[kv, j]).start()
+
+            @pl.when(jnp.logical_not(local))
+            def _():
+                remote(
+                    src, dst, s1s.at[kv, j], s1r.at[kv, x], j * 8 + z * 2 + core, role_head
+                ).start()
+
+    def q_copy(t):
+        j = (x + 4 - t) % 4
+        return (
+            q_cross.at[:, pl.ds(j * GC, GC)], qb.at[x], qs.at[t], qr.at[x],
+            j * 8 + z * 2 + core, role_head,
+        )
+
+    def q_start(t):
+        src, dst, ssem, rsem, cc, hh = q_copy(t)
+        if t == 0:
+            @pl.when(mixed)
+            def _():
+                pltpu.make_async_copy(src, dst, rsem).start()
+
+            @pl.when(jnp.logical_not(mixed))
+            def _():
+                remote(src, dst, ssem, rsem, cc, hh).start()
+        else:
+            remote(src, dst, ssem, rsem, cc, hh).start()
+
+    def z_copy(kv, step):
+        if step == 2:
+            tile, to = ((z + 1) % 4, (z + 3) % 4) if kv == 0 else ((z + 3) % 4, (z + 1) % 4)
+        else:
+            tile, to = z, (z + 1 + 2 * step) % 4
+        part = (kb, vb)[kv].at[tile, :, pl.ds(core * TOK, TOK), :]
+        return remote(
+            part, part, zs.at[kv, step], zr.at[kv, step], x * 8 + to * 2 + yh, h
+        )
+
+    def z_of(n):
+        return (z + jnp.where(n == 1, 1, jnp.where(n == 2, 3, jnp.where(n == 3, 2, 0)))) % 4
+
+    def b_copy(kv, n):
+        part = (kb, vb)[kv].at[z_of(n), :, pl.ds(core * TOK, TOK), :]
+        return remote(part, part, bs.at[kv, n], br.at[kv, n], c, h + 1 - 2 * core)
+
+    def b_start(n):
+        for kv in range(2):
+            if n > 0:
+                z_copy(kv, (1, 0, 2)[n - 1]).wait_recv()
+            b_copy(kv, n).start()
+        if n in (1, 2):
+            z_copy(n - 1, 2).start()
+
+    def b_wait(n):
+        for kv in range(2):
+            b_copy(kv, n).wait_recv()
+
+    def own_chunk():
+        for kv in range(2):
+            for j in range(4):
+                part = (kb, vb)[kv].at[z, j, pl.ds(core * TOK, TOK), :]
+                remote(part, part, s1s.at[kv, 0], s1r.at[kv, j], c, h).wait_recv()
+            for step in (0, 1):
+                z_copy(kv, step).start()
+        b_start(0)
+
+    def w_copy(kv):
+        return remote(
+            (k_win, v_win)[kv], (wk, wv)[kv].at[0], ws.at[kv, 0], wr.at[kv, 0], c + 2, h
+        )
+
+    def w_start():
+        for kv in range(2):
+            @pl.when(c + 2 < CTX)
+            def _():
+                w_copy(kv).start()
+
+    def y_copy(kv, slot):
+        ref = (wk, wv)[kv]
+        return remote(ref.at[slot], ref.at[1], ws.at[kv, 1], wr.at[kv, 1], partner(0), h)
+
+    def w_arrive():
+        for kv in range(2):
+            ref = (wk, wv)[kv]
+
+            @pl.when(c >= 2)
+            def _():
+                w_copy(kv).wait_recv()
+
+            @pl.when(c < 2)
+            def _():
+                ref[0] = jnp.zeros((TOK, GROUPS * D), bf16)
+
+            @pl.when(yh == 1)
+            def _():
+                y_copy(kv, 0).start()
+
+    w_start()
+    q_start(0)
+
     hot = (lax.broadcasted_iota(jnp.int32, (64, TOK), 0) == index[...]).astype(f32)
     lw[...] = dot(hot, table[...], 0, 0, lax.Precision.HIGHEST)
 
@@ -110,144 +243,11 @@
                 s, vl[:, g * D : (g + 1) * D], 1, 0
             )
 
-    pl.semaphore_wait(
-        barrier,
-        jnp.where(mixed, 3, 6) + 7 + jnp.where((z == 0) | (z == 3), 1, 0),
-    )
-
-    def s1_copy(j, kv):
-        src = (k_sh, v_sh)[kv].at[:, pl.ds(j * D, D)]
-        dst = (kb, vb)[kv].at[z, x, pl.ds(yh * TOK, TOK), :]
-        return src, dst
-
-    def f_copy(level):
-        return remote(
-            fs.at[level], fr.at[level], fss.at[level], frs.at[level], partner(level), h
-        )
-
-    def fenwick(level):
-        f_copy(level).wait_recv()
-        got = fr[level]
-        if level < 4:
-            total = state[...] + got.astype(f32)
-            state[...] = total
-            fs[level + 1] = total.astype(bf16)
-            f_copy(level + 1).start()
-
-    f_copy(0).start()
-
-    for j in range(4):
-        for kv in range(2):
-            src, dst = s1_copy(j, kv)
-            local = mixed & (x == j)
-
-            @pl.when(local)
-            def _():
-                pltpu.make_async_copy(src, dst, s1r.at[kv, j]).start()
-
-            @pl.when(jnp.logical_not(local))
-            def _():
-                remote(
-                    src, dst, s1s.at[kv, j], s1r.at[kv, x], j * 8 + z * 2 + core, role_head
-                ).start()
-
-    def q_copy(t):
-        j = (x + 4 - t) % 4
-        return (
-            q_cross.at[:, pl.ds(j * GC, GC)], qb.at[x], qs.at[t], qr.at[x],
-            j * 8 + z * 2 + core, role_head,
-        )
-
-    def q_start(t):
-        src, dst, ssem, rsem, cc, hh = q_copy(t)
-        if t == 0:
-            @pl.when(mixed)
-            def _():
-                pltpu.make_async_copy(src, dst, rsem).start()
-
-            @pl.when(jnp.logical_not(mixed))
-            def _():
-                remote(src, dst, ssem, rsem, cc, hh).start()
-        else:
-            remote(src, dst, ssem, rsem, cc, hh).start()
-
-    def z_copy(kv, step):
-        if step == 2:
-            tile, to = ((z + 1) % 4, (z + 3) % 4) if kv == 0 else ((z + 3) % 4, (z + 1) % 4)
-        else:
-            tile, to = z, (z + 1 + 2 * step) % 4
-        part = (kb, vb)[kv].at[tile, :, pl.ds(core * TOK, TOK), :]
-        return remote(
-            part, part, zs.at[kv, step], zr.at[kv, step], x * 8 + to * 2 + yh, h
-        )
-
-    def z_of(n):
-        return (z + jnp.where(n == 1, 3, jnp.where(n == 2, 1, jnp.where(n == 3, 2, 0)))) % 4
-
-    def b_copy(kv, n):
-        part = (kb, vb)[kv].at[z_of(n), :, pl.ds(core * TOK, TOK), :]
-        return remote(part, part, bs.at[kv, n], br.at[kv, n], c, h + 1 - 2 * core)
-
-    def b_start(n):
-        for kv in range(2):
-            if n > 0:
-                z_copy(kv, n - 1).wait_recv()
-            b_copy(kv, n).start()
-        if n == 1:
-            z_copy(1, 2).start()
-        if n == 2:
-            z_copy(0, 2).start()
-
-    def b_wait(n):
-        for kv in range(2):
-            b_copy(kv, n).wait_recv()
-
-    def own_chunk():
-        for kv in range(2):
-            for j in range(4):
-                part = (kb, vb)[kv].at[z, j, pl.ds(core * TOK, TOK), :]
-                remote(part, part, s1s.at[kv, 0], s1r.at[kv, j], c, h).wait_recv()
-            for step in (0, 1):
-                z_copy(kv, step).start()
-        b_start(0)
-
-    def w_copy(kv):
-        return remote(
-            (k_win, v_win)[kv], (wk, wv)[kv].at[0], ws.at[kv, 0], wr.at[kv, 0], c + 2, h
-        )
-
-    def w_start():
-        for kv in range(2):
-            @pl.when(c + 2 < CTX)
-            def _():
-                w_copy(kv).start()
-
-    def y_copy(kv, slot):
-        ref = (wk, wv)[kv]
-        return remote(ref.at[slot], ref.at[1], ws.at[kv, 1], wr.at[kv, 1], partner(0), h)
-
-    def w_arrive():
-        for kv in range(2):
-            ref = (wk, wv)[kv]
-
-            @pl.when(c >= 2)
-            def _():
-                w_copy(kv).wait_recv()
-
-            @pl.when(c < 2)
-            def _():
-                ref[0] = jnp.zeros((TOK, GROUPS * D), bf16)
-
-            @pl.when(yh == 1)
-            def _():
-                y_copy(kv, 0).start()
-
-    w_start()
-    q_start(0)
+    fenwick(0)
+    fenwick(1)
     own_chunk()
     for t in range(1, 4):
         q_start(t)
-    fenwick(0)
     for i in (3, 4, 5):
         loads[i].wait()
 
@@ -312,13 +312,15 @@
 
     events = {
         0: [lambda: b_wait(0)],
-        1: [lambda: fenwick(1)],
+        1: [lambda: fenwick(2)],
         2: [w_y_start],
-        3: [lambda: fenwick(2), w_arrive],
-        4: [lambda: b_start(1), lambda: b_start(2), lambda: b_wait(1)],
-        6: [lambda: fenwick(3)],
+        3: [w_arrive],
+        4: [lambda: b_start(1), lambda: b_wait(1)],
+        5: [lambda: fenwick(3)],
+        6: [lambda: b_start(2)],
         8: [lambda: b_wait(2)],
-        10: [lambda: fenwick(4), lambda: b_start(3)],
+        9: [lambda: fenwick(4)],
+        10: [lambda: b_start(3)],
         12: [lambda: b_wait(3)],
     }
 

time: 89.6 us -> 88.7 us (0.990)
  no operation moved by 1% of the time
where the time goes in v4:
time: 88.7 us; the launch traced here: 88.1 us
  Pallas kernels  84.3 us (95%)
  local copies, waits for them, and re-layouts  3.83 us (4%)
    pallas_call x1, Pallas kernels, per_device(): pl.pallas_call(kernel, out_shape=jax.ShapeDtypeStruct((TOK, HEADS * D), b...  84.3 us
    unnamed x2, local copies, waits for them, and re-layouts  3.12 us

profile of v4, /device:TPU:97, one launch (start us, length us, event | category | flops | bytes accessed | tf_op | source)
XLA Modules:
  0.0 88.1 jit_solution(2449187776184601791)
XLA Ops:
  0.0 0.8 copy.14
  0.8 0.7 copy.15.table
  1.5 84.3 %hybrid_attention.1 = bf16[256,2048]{1,0:T(8,128)(2,1)} custom-call(bf16[256,2048]{1,0:T(8,128)(2,1)} %q_win.1, bf16[256,512]{1,0:T(8,128)(2,1)} %k_win.1, bf16[256,512]{1,0:T(8,128)(2,1)} %v_win.1, bf16[256,2048]{1,0:T(8,128)(2,1)} %q_lin.1, bf16[256,512]{1,0:T(8,128)(2,1)} %k_lin.1, bf16[256,512]{1,0:T(8,128)(2,1)} %v_lin.1, f32[64,96]{1,0:T(8,128)} %copy.15.table, ...), custom_call_target="tpu_custom_call" | custom-call | tf_op jit(solution)/shard_map/hybrid_attention/pallas_call | solution.py:469
  85.8 2.3 %copy.17 = bf16[256,2048]{1,0:T(8,128)(2,1)} copy(bf16[256,2048]{1,0:T(8,128)(2,1)} %hybrid_attention.1) | data formatting | bytes 2097152
  (1 shorter events, 0.0 us)

commit v5 on v4

--- a/solution.py
+++ b/solution.py
@@ -50,9 +50,6 @@
         (k_lin, kl), (v_lin, vl), (q_lin, ql), (k_win, wk.at[2]), (v_win, wv.at[2]), (q_win, qw),
     ]
     loads = [pltpu.make_async_copy(s, d, in_sem.at[i]) for i, (s, d) in enumerate(loads)]
-    for copy in loads:
-        copy.start()
-
     barrier = pltpu.get_barrier_semaphore()
 
     def greet(cc, hh):
@@ -86,6 +83,9 @@
     @pl.when(z == 0)
     def _():
         greet((c + CTX - 2) % CTX, h)
+
+    for copy in loads:
+        copy.start()
 
     loads[0].wait()
     loads[1].wait()
@@ -228,7 +228,7 @@
     q_start(0)
 
     hot = (lax.broadcasted_iota(jnp.int32, (64, TOK), 0) == index[...]).astype(f32)
-    lw[...] = dot(hot, table[...], 0, 0, lax.Precision.HIGHEST)
+    lw[...] = dot(hot, table[...].reshape(LEVELS * HEADS, 64), 0, 1, lax.Precision.HIGHEST)
 
     loads[2].wait()
     rows = lax.broadcasted_iota(jnp.int32, (TOK, TOK), 0)
@@ -239,7 +239,7 @@
             hd = g * PER + r
             s = dot(ql[:, hd * D : (hd + 1) * D], kl[:, g * D : (g + 1) * D], 1, 1)
             s = jnp.where(causal, s * (D * TOK) ** -0.5, 0.0).astype(bf16)
-            comb[:, hd * D : (hd + 1) * D] = lw[:, hd * LEVELS : hd * LEVELS + 1] * dot(
+            comb[:, hd * D : (hd + 1) * D] = lw[:, hd : hd + 1] * dot(
                 s, vl[:, g * D : (g + 1) * D], 1, 0
             )
 
@@ -367,7 +367,7 @@
             for r in range(PER):
                 hd = g * PER + r
                 term = dot(ql[:, hd * D : (hd + 1) * D], bucket, 1, 0)
-                at = hd * LEVELS + level + 1
+                at = (level + 1) * HEADS + hd
                 comb[:, hd * D : (hd + 1) * D] += (lw[:, at : at + 1] * scale) * term
 
     for kv in range(2):
@@ -486,7 +486,7 @@
             pltpu.VMEM((4, PER * TOK, 2 * D), f32),
             pltpu.VMEM((4, PER * TOK, D), f32),
             pltpu.VMEM((TOK, HEADS * D), f32),
-            pltpu.VMEM((TOK, HEADS * LEVELS), f32),
+            pltpu.VMEM((TOK, LEVELS * HEADS), f32),
             pltpu.VMEM((GROUPS, D, D), f32),
             pltpu.VMEM((5, GROUPS, D, D), bf16),
             pltpu.VMEM((5, GROUPS, D, D), bf16),
@@ -508,7 +508,7 @@
         name="hybrid_attention",
     )(
         q_win, k_win, v_win, q_lin, k_lin, v_lin,
-        level_table.reshape(level_table.shape[0], -1), level_index.reshape(1, -1),
+        level_table.transpose(2, 1, 0), level_index.reshape(1, -1),
         q_cross, k_shared, v_shared, head_gain,
     )
 

time: 88.7 us -> 87 us (0.981)
  local copies, waits for them, and re-layouts: 3.83 us -> 2.3 us
    unnamed x2 -> x1, local copies, waits for them, and re-layouts: 3.12 us -> 2.3 us
where the time goes in v5:
time: 87 us; the launch traced here: 86.6 us
  Pallas kernels  84.3 us (97%)
  local copies, waits for them, and re-layouts  2.3 us (3%)
    pallas_call x1, Pallas kernels, per_device(): pl.pallas_call(kernel, out_shape=jax.ShapeDtypeStruct((TOK, HEADS * D), b...  84.3 us
    unnamed x1, local copies, waits for them, and re-layouts  2.3 us

profile of v5, /device:TPU:97, one launch (start us, length us, event | category | flops | bytes accessed | tf_op | source)
XLA Modules:
  0.0 86.6 jit_solution(155113956063933103)
XLA Ops:
  0.0 84.3 %hybrid_attention.1 = bf16[256,2048]{1,0:T(8,128)(2,1)} custom-call(bf16[256,2048]{1,0:T(8,128)(2,1)} %q_win.1, bf16[256,512]{1,0:T(8,128)(2,1)} %k_win.1, bf16[256,512]{1,0:T(8,128)(2,1)} %v_win.1, bf16[256,2048]{1,0:T(8,128)(2,1)} %q_lin.1, bf16[256,512]{1,0:T(8,128)(2,1)} %k_lin.1, bf16[256,512]{1,0:T(8,128)(2,1)} %v_lin.1, f32[6,16,64]{2,1,0:T(8,128)} %bitcast.2, ...), custom_call_target="tpu_custom_call" | custom-call | tf_op jit(solution)/shard_map/hybrid_attention/pallas_call | solution.py:469
  84.3 2.3 %copy.14 = bf16[256,2048]{1,0:T(8,128)(2,1)} copy(bf16[256,2048]{1,0:T(8,128)(2,1)} %hybrid_attention.1) | data formatting | bytes 2097152

commit v6 on v5

--- a/solution.py
+++ b/solution.py
@@ -244,8 +244,8 @@
             )
 
     fenwick(0)
+    own_chunk()
     fenwick(1)
-    own_chunk()
     for t in range(1, 4):
         q_start(t)
     for i in (3, 4, 5):

time: 87 us -> 87.8 us (level)
  no operation moved by 1% of the time
where the time goes in v6:
time: 87.8 us; the launch traced here: 86.6 us
  Pallas kernels  84.3 us (96%)
  local copies, waits for them, and re-layouts  2.3 us (3%)
    pallas_call x1, Pallas kernels, per_device(): pl.pallas_call(kernel, out_shape=jax.ShapeDtypeStruct((TOK, HEADS * D), b...  84.3 us
    unnamed x1, local copies, waits for them, and re-layouts  2.3 us

profile of v6, /device:TPU:97, one launch (start us, length us, event | category | flops | bytes accessed | tf_op | source)
XLA Modules:
  0.0 86.6 jit_solution(15001725115046238881)
XLA Ops:
  0.0 84.3 %hybrid_attention.1 = bf16[256,2048]{1,0:T(8,128)(2,1)} custom-call(bf16[256,2048]{1,0:T(8,128)(2,1)} %q_win.1, bf16[256,512]{1,0:T(8,128)(2,1)} %k_win.1, bf16[256,512]{1,0:T(8,128)(2,1)} %v_win.1, bf16[256,2048]{1,0:T(8,128)(2,1)} %q_lin.1, bf16[256,512]{1,0:T(8,128)(2,1)} %k_lin.1, bf16[256,512]{1,0:T(8,128)(2,1)} %v_lin.1, f32[6,16,64]{2,1,0:T(8,128)} %bitcast.2, ...), custom_call_target="tpu_custom_call" | custom-call | tf_op jit(solution)/shard_map/hybrid_attention/pallas_call | solution.py:469
  84.3 2.3 %copy.14 = bf16[256,2048]{1,0:T(8,128)(2,1)} copy(bf16[256,2048]{1,0:T(8,128)(2,1)} %hybrid_attention.1) | data formatting | bytes 2097152
